TPU v7x, 256 devices: a whole 4x4x8 slice. The times are simulated.
256 devices in a mesh: ps: 64 (over y, z_hi, x), patch: 4 (over z_lo, core).
Axes of the slice: x: 4, y: 4, z: 8 (z_hi: 4, z_lo: 2; z = z_hi * 2 + z_lo), core: 2. Of those that a mesh axis runs over, the one named last changes fastest.
Arguments:
- tiles: bfloat16 [64, 4, 256, 128, 128], P('ps', 'patch'), may hold values from -0.109375 to 0.109375
- tile_row: int32 [64, 4, 256], P('ps', 'patch'), may hold values from 0 to 15
- tile_col: int32 [64, 4, 256], P('ps', 'patch'), may hold values from 0 to 31
- tile_count: int32 [64, 4], P('ps', 'patch'), may hold values from 32 to 256, as said below
- slip: bfloat16 [48, 16384], P(None, 'patch'), may hold values from -6 to 6
- observations: float32 [48, 131072], P(None, 'ps'), may hold values from -6 to 6
- edge_list: int32 [2, 32768], replicated, may hold values from 0 to 16383, as said below
Outputs:
- residual: float32 [48, 131072], P(None, 'ps')
- gradient: float32 [48, 16384], P(None, ('patch', 'ps'))
Inputs may be any that keep to these rules, and one draw needn't show every extreme that they name: `tile_count`: each ps index holds 256 live slots on every patch index in some draws and each draw has one such ps index; the others hold between 32 and 128. `edge_list`: edges 2 p and 2 p + 1 both have patch p as one of their ends, first or second; the other end lies 1 to 256 patches before or after p, counted cyclically over 16384; the distance 256 occurs.
All inputs are finite; a program needn't handle non-finite values.
Results may differ from a plain program's by a relative error of at most 0.0013.
Values may be sent and summed in bfloat16 or wider, within the bound.
A program may use at most 128 MiB of HBM per device.

v0:
```python
import jax
import jax.numpy as jnp
from jax import lax
from jax.sharding import PartitionSpec as P

GROUP = 16
REACH = 256


HIGH = lax.Precision.HIGHEST


def padded(shard, sides, width):
    for axis, dim in sides:
        size, length = (lax.axis_size(axis), shard.shape[dim])
        up = [(i, (i + 1) % size) for i in range(size)]
        down = [(j, i) for i, j in up]
        last = lax.slice_in_dim(shard, length - width, length, axis=dim)
        initial = lax.slice_in_dim(shard, 0, width, axis=dim)
        before = lax.ppermute(last, axis, up)
        after = lax.ppermute(initial, axis, down)
        shard = jnp.concatenate([before, shard, after], axis=dim)
    return shard


def tile_loop(count, step_fn, start):
    trips = (count + GROUP - 1) // GROUP
    return lax.fori_loop(0, trips, step_fn, start)


def cyclic_slice(array, start, length):
    extended = jnp.concatenate([array, array[:, :length]], axis=1)
    return lax.dynamic_slice_in_dim(extended, start, length, 1)


def incidence(edges, root, patches_all, width):
    local_first = (edges[0] - root) % patches_all
    local_second = (edges[1] - root) % patches_all
    columns = jnp.arange(width, dtype=jnp.int32)[None, :]
    hits = (local_first[:, None] == columns).astype(jnp.float32)
    return hits - (local_second[:, None] == columns).astype(jnp.float32)


def body(tiles, tile_row, tile_col, tile_count, slip, observations, edge_list):
    tile_dev = tiles[0, 0]
    row_dev = tile_row[0, 0]
    col_dev = tile_col[0, 0]
    count = tile_count[0, 0]
    block = tile_dev.shape[-1]
    dates = slip.shape[0]
    k_dev = slip.shape[1]
    kb_dev = k_dev // block
    rows_dev = observations.shape[1]
    pb_dev = rows_dev // block
    slip_blocks = slip.reshape(dates, kb_dev, block)

    def pieces(start):
        tl = lax.dynamic_slice_in_dim(tile_dev, start, GROUP, 0)
        rw = lax.dynamic_slice_in_dim(row_dev, start, GROUP, 0)
        cl = lax.dynamic_slice_in_dim(col_dev, start, GROUP, 0)
        live = start + jnp.arange(GROUP) < count
        return (tl, rw, cl, live)

    def forward_step(group, acc):
        tl, rw, cl, live = pieces(group * GROUP)
        picked = jnp.take(slip_blocks, cl, axis=1)
        prod = jnp.einsum("tpk,dtk->tdp", tl, picked, preferred_element_type=jnp.float32)
        row_hot = ((rw[:, None] == jnp.arange(pb_dev)[None, :]) & live[:, None]).astype(jnp.float32)
        return acc + jnp.einsum("tr,tdp->drp", row_hot, prod, precision=HIGH)

    partial_value = tile_loop(count, forward_step, jnp.zeros((dates, pb_dev, block), jnp.float32))
    predicted = lax.psum(partial_value.reshape(dates, rows_dev), "patch")
    residual = predicted - observations
    resid_blocks = residual.astype(jnp.bfloat16).reshape(dates, pb_dev, block)
    part_dates = resid_blocks.shape[0]

    def back_step(group, acc):
        tl, rw, cl, live = pieces(group * GROUP)
        picked = jnp.take(resid_blocks, rw, axis=1)
        prod = jnp.einsum("tpk,dtp->tdk", tl, picked, preferred_element_type=jnp.float32)
        col_hot = ((cl[:, None] == jnp.arange(kb_dev)[None, :]) & live[:, None]).astype(jnp.float32)
        return acc + jnp.einsum("tc,tdk->dck", col_hot, prod, precision=HIGH)

    total = tile_loop(count, back_step, jnp.zeros((part_dates, kb_dev, block), jnp.float32))
    data_grad = lax.psum_scatter(
        total.reshape(part_dates, k_dev), "ps", scatter_dimension=1, tiled=True
    )
    share = data_grad.shape[1]
    patches_all = k_dev * lax.axis_size("patch")
    own_start = lax.axis_index("patch") * k_dev + lax.axis_index("ps") * share
    outer_width = share + 8 * REACH
    margin = 4 * REACH
    extended = padded(slip, (("patch", 1),), margin)
    window = lax.dynamic_slice_in_dim(extended, lax.axis_index("ps") * share, outer_width, 1)
    edges_all = edge_list.shape[1]
    outer_edges = cyclic_slice(
        edge_list, 2 * (own_start - 3 * REACH) % edges_all, 2 * (share + 6 * REACH)
    )
    outer_map = incidence(outer_edges, own_start - 4 * REACH, patches_all, outer_width)
    outer_diff = jnp.dot(
        window, outer_map.astype(jnp.bfloat16).T, preferred_element_type=jnp.float32
    )
    smooth = jnp.dot(outer_diff, outer_map, precision=HIGH, preferred_element_type=jnp.float32)
    inner_width = share + 4 * REACH
    smooth_mid = smooth[:, 2 * REACH : 2 * REACH + inner_width]
    inner_edges = cyclic_slice(
        edge_list, 2 * (own_start - REACH) % edges_all, 2 * (share + 2 * REACH)
    )
    inner_map = incidence(inner_edges, own_start - 2 * REACH, patches_all, inner_width)
    inner_diff = jnp.dot(
        smooth_mid, inner_map.T, precision=HIGH, preferred_element_type=jnp.float32
    )
    curvature = jnp.dot(inner_diff, inner_map, precision=HIGH, preferred_element_type=jnp.float32)
    own_curve = curvature[:, 2 * REACH : 2 * REACH + share]
    gradient = data_grad + 0.05 * own_curve
    return (residual, gradient)


def solution(mesh):
    in_specs = (
        P("ps", "patch", None, None, None),
        P("ps", "patch", None),
        P("ps", "patch", None),
        P("ps", "patch"),
        P(None, "patch"),
        P(None, "ps"),
        P(),
    )
    out_specs = (P(None, "ps"), P(None, ("patch", "ps")))
    return jax.shard_map(body, mesh=mesh, in_specs=in_specs, out_specs=out_specs, check_vma=False)
```

profile of v0, /device:TPU:32, one launch (start us, length us, event | category | flops | bytes accessed | tf_op | source)
XLA Modules:
  0.0 580.7 jit_solution(13806673855705868550)
XLA Ops:
  7.2 1.0 fusion.52
  8.3 1.7 collective-permute-start.1
  10.6 1.1 copy_bitcast_fusion.1
  11.8 29.2 %while.20 = (s32[]{:T(128)}, f32[48,16,128]{2,1,0:T(8,128)S(1)}, s32[]{:T(128)}, s32[256]{0:T(256)}, bf16[48,32,128]{2,0,1:T(8,128)(2,1)S(1)}, /*index=5*/bf16[2...) while((s32[]{:T(128)}, f32[48,16,128]{2,1,0:T(8,128)S(1)}, ...), condition=%wide.region_1.2_spmd, body=%wide.region_0.1_spmd.sunk | while | flops 44238468 | bytes 2691767 | solution.py:28
  11.8 1.4 compare_and_fusion.4
  13.9 1.6 fusion.73
  15.4 0.8 dynamic_slice.76
  16.7 1.4 compare_and_fusion.4
  18.7 1.6 fusion.73
  20.3 0.8 dynamic_slice.76
  21.6 1.4 compare_and_fusion.4
  23.6 1.6 fusion.73
  25.1 0.8 dynamic_slice.76
  26.4 1.4 compare_and_fusion.4
  28.4 1.6 fusion.73
  30.0 0.8 dynamic_slice.76
  31.3 1.4 compare_and_fusion.4
  33.3 1.6 fusion.73
  34.8 0.8 dynamic_slice.76
  36.1 1.4 compare_and_fusion.4
  38.1 1.6 fusion.73
  39.7 0.8 dynamic_slice.76
  41.0 0.9 copy.31
  42.3 10.2 %convert_subtract_fusion = f32[3200,2112]{1,0:T(8,128)} fusion(s32[3200]{0:T(1024)S(1)} %get-tuple-element.176, s32[3200]{0:T(1024)S(1)} %get-tuple-element.177), kind=kLoop, calls=%fused_computation.42 | loop fusion | flops 33792000 | bytes 27059200 | tf_op jit(solution)/shard_map/sub | solution.py:41
  52.7 3.0 convert_subtract_fusion.2
  55.6 73.1 %all-reduce.2.cloned.1.call-done = f32[48,2048]{1,0:T(8,128)} async-done(((f32[48,2048]{1,0:T(8,128)}), f32[48,2048]{1,0:T(8,128)}) %all-reduce.2.cloned.1.call-update) | async-done | bytes 393232 | tf_op jit(solution)/shard_map/psum | solution.py:72
  128.7 1.8 convert_bitcast_fusion
  130.7 21.6 %while.21 = (s32[]{:T(128)}, f32[48,32,128]{2,1,0:T(8,128)S(1)}, s32[]{:T(128)}, s32[256]{0:T(256)S(1)}, bf16[48,16,128]{2,0,1:T(8,128)(2,1)S(1)}, /*index=5*/bf...) while((s32[]{:T(128)}, f32[48,32,128]{2,1,0:T(8,128)S(1)}, ...), condition=%wide.region_4.5_spmd, body=%wide.region_3.4_spmd.sunk | while | flops 63211652 | bytes 3478199 | solution.py:28
  130.7 0.8 compare_and_fusion.5
  132.1 1.4 fusion.79
  133.6 0.7 fusion.80
  135.7 1.4 fusion.79
  137.1 0.7 fusion.80
  139.2 1.4 fusion.79
  140.7 0.7 fusion.80
  142.8 1.4 fusion.79
  144.2 0.7 fusion.80
  146.3 1.4 fusion.79
  147.8 0.7 fusion.80
  149.9 1.4 fusion.79
  151.4 0.7 fusion.80
  152.3 2.0 copy.20
  154.3 7.3 %fusion.32 = f32[48,3200]{1,0:T(8,128)S(1)} fusion(s32[3200]{0:T(1024)S(1)} %get-tuple-element.176, s32[3200]{0:T(1024)S(1)} %get-tuple-element.177, s32[]{:T(128)S(6)} %select_n.89, bf16[48,1024]{1,0:T(8,128)(2,1)S(1)} %collective-permute-done, bf16[48,4096]{1,0:T(8,128)(2,1)S(1)} %copy-done.1, bf16[48,1024]{1,0:T(8,128)(2,1)S(1)} %collective-permute-done.1), kind=kOutput, calls=%fused_computation.47 | convolution fusion | flops 689965056 | bytes 1229828 | tf_op jit(solution)/shard_map/dot_general | solution.py:100
  161.6 11.7 %fusion.30 = f32[48,1088]{1,0:T(8,128)S(1)} fusion(f32[48,3200]{1,0:T(8,128)S(1)} %fusion.32, f32[3200,2112]{1,0:T(8,128)} %convert_subtract_fusion), kind=kOutput, calls=%fused_computation.45 | convolution fusion | flops 2005401600 | bytes 15568896 | tf_op jit(solution)/shard_map/dot_general | solution.py:103
  173.3 5.4 fusion.34
  178.8 392.1 %reduce-scatter.4.cloned.1.call-done = f32[64,48]{1,0:T(8,128)} async-done(((f32[4096,48]{1,0:T(8,128)}), f32[64,48]{1,0:T(8,128)}) %reduce-scatter.4.cloned.1.call-update) | async-done | bytes 12304
  570.9 0.8 copy.19
  571.7 2.1 fusion.35
  (71 shorter events, 15.0 us)
Async XLA Ops:
  7.2 121.6 %all-reduce.2.cloned.1.call-start = ((), (), s32[]{:S(2)}) async-start(), calls=%async_computation.1 | async-start | bytes 786432 | tf_op jit(solution)/shard_map/psum | solution.py:72
  8.2 146.1 %collective-permute-start = (bf16[48,1024]{1,0:T(8,128)(2,1)S(1)}, bf16[48,1024]{1,0:T(8,128)(2,1)S(1)}, u32[]{:S(2)}, u32[]{:S(2)}) collective-permute-start(bf16[48,1024]{1,0:T(8,128)(2,1)S(1)} %get-tuple-element.175), channel_id=1, source_target_pairs={{0,1},{1,2},{2,3},{3,0},{4,5},{5,6},{6,7},{7,4},{8,9},{9,10},{10,1... | collective-permute-start | bytes 294920 | tf_op jit(solution)/shard_map/ppermute | solution.py:20
  8.3 146.0 %collective-permute-start.1 = (bf16[48,1024]{1,0:T(8,128)(2,1)S(1)}, bf16[48,1024]{1,0:T(8,128)(2,1)S(1)}, u32[]{:S(2)}, u32[]{:S(2)}) collective-permute-start(bf16[48,1024]{1,0:T(8,128)(2,1)S(1)} %get-tuple-element.174), channel_id=1, source_target_pairs={{1,0},{2,1},{3,2},{0,3},{5,4},{6,5},{7,6},{4,7},{9,8},{10,9},{11,1... | collective-permute-start | bytes 294920 | tf_op jit(solution)/shard_map/ppermute | solution.py:21
  11.8 30.2 %copy-start = (s32[2,32768]{1,0:T(2,128)S(1)}, s32[2,32768]{1,0:T(2,128)}, u32[]{:S(2)}) copy-start(s32[2,32768]{1,0:T(2,128)} %param.17) | copy-start | bytes 786436
  11.8 30.2 %slice-start = ((s32[2,32768]{1,0:T(2,128)}), s32[2,3200]{1,0:T(2,128)S(1)}, s32[]{:S(2)}) async-start(s32[2,32768]{1,0:T(2,128)} %param.17), calls=%async_computation.3 | async-start | bytes 51200 | tf_op jit(solution)/shard_map/slice | solution.py:32
  41.9 529.0 %reduce-scatter.4.cloned.1.call-start = ((), (), s32[]{:S(2)}) async-start(), calls=%async_computation.2 | async-start | bytes 2129920
  42.3 10.2 %slice-start.1 = ((s32[2,32768]{1,0:T(2,128)}), s32[2,1152]{1,0:T(2,128)S(1)}, s32[]{:S(2)}) async-start(s32[2,32768]{1,0:T(2,128)} %param.17), calls=%async_computation.4 | async-start | bytes 18432 | tf_op jit(solution)/shard_map/slice | solution.py:32
  42.3 86.5 %copy-start.2 = (f32[48,2048]{1,0:T(8,128)S(1)}, f32[48,2048]{1,0:T(8,128)}, u32[]{:S(2)}) copy-start(f32[48,2048]{1,0:T(8,128)} %param.16) | copy-start | bytes 1179652
  52.5 78.2 %copy-start.3 = (s32[256]{0:T(256)S(1)}, s32[256]{0:T(256)}, u32[]{:S(2)}) copy-start(s32[256]{0:T(256)} %get-tuple-element.375) | copy-start | bytes 3076
  52.5 78.2 %copy-start.4 = (s32[256]{0:T(256)S(1)}, s32[256]{0:T(256)}, u32[]{:S(2)}) copy-start(s32[256]{0:T(256)} %get-tuple-element.376) | copy-start | bytes 3076
  130.7 23.6 %copy-start.1 = (bf16[48,4096]{1,0:T(8,128)(2,1)S(1)}, bf16[48,4096]{1,0:T(8,128)(2,1)}, u32[]{:S(2)}) copy-start(bf16[48,4096]{1,0:T(8,128)(2,1)} %param.15) | copy-start | bytes 1179652
Sparse Core Ops, SparseCore 0:
  42.0 86.7 all-reduce.1
  154.4 416.4 reduce-scatter.3
where the time goes:
time: 583 us; the launch traced here: 581 us
  waiting for transfers between devices  465 us (80%)
  matrix products  51.6 us (9%)
  other arithmetic  28.3 us (5%)
  local copies, waits for them, and re-layouts  17.9 us (3%)
  between operations  15 us (3%)
    unnamed x3, waiting for transfers between devices  392 us
    psum x1, waiting for transfers between devices, body(): predicted = lax.psum(partial_value.reshape(dates, rows_dev), 'patch')  73.1 us
    sub x2, other arithmetic, incidence(): return hits - (local_second[:, None] == columns).astype(jnp.float32)  13.2 us
    dot_general x1, matrix products, body(): jnp.dot(outer_diff, outer_map, precision=HIGH, preferred_element_type=jnp...  11.7 us
  transfers between devices with their start and end apart: 4, of which 2 were waited for; matrix products, arithmetic and copies ran while one was open for 16% of the time, Pallas kernels for 0%

commit v1 on v0

v1 whole, which is shorter than its diff:
```python
import jax
import jax.numpy as jnp
from jax import lax
from jax.experimental import pallas as pl
from jax.experimental.pallas import tpu as pltpu
from jax.sharding import PartitionSpec as P

F32 = jnp.float32
BF16 = jnp.bfloat16
MESH = pl.DeviceIdType.MESH

BLOCK = 128
DATES = 48
SLOTS = 256
CHUNKS = 4
CH = SLOTS // CHUNKS
ROWS = 16
COLS = 32
HALF = ROWS // 2 * BLOCK
K_DEV = COLS * BLOCK
HALO = 4
WIN = 2 * HALO + 1
PATCHES = 16384
UNROLL = 8


def xor(value, m):
    if m == 0:
        return value
    if m == 1:
        return value + 1 - 2 * (value % 2)
    if m == 2:
        return (value + 2) % 4
    return 3 - value


def iota(shape, dim):
    return lax.broadcasted_iota(jnp.int32, shape, dim)


def sort_slots(row_ref, col_ref, count_ref, order, same, ends):
    shape = (SLOTS, SLOTS)
    t_lane = iota((1, SLOTS), 1)
    live = t_lane < count_ref[...]
    row = row_ref[0]
    col = col_ref[0]
    chunk_f = (t_lane // CH).astype(F32)
    t_f = t_lane.astype(F32)
    diagonal = iota(shape, 0) == iota(shape, 1)
    lane_f = iota(shape, 1).astype(F32)
    which = iota((16, SLOTS), 0)
    picker = (iota((SLOTS, 128), 0) // CH == iota((SLOTS, 128), 1)).astype(BF16)
    chunk_at = iota((COLS, 128), 1)
    for n, (mine, other, dead, limit) in enumerate(((row, col, ROWS, COLS - 1), (col, row, COLS, ROWS - 1))):
        own = jnp.where(live, mine, dead).astype(F32)
        key = (chunk_f * 64.0 + own) * SLOTS + t_f
        key_col = jnp.sum(jnp.where(diagonal, key, 0.0), axis=1, keepdims=True)
        rank = jnp.sum(jnp.where(key < key_col, 1.0, 0.0), axis=1, keepdims=True)
        one_hot = jnp.where(rank == lane_f, 1.0, 0.0).astype(BF16)
        values = jnp.where(which == 0, t_f - chunk_f * CH, jnp.where(which == 1, other.astype(F32), own))
        ordered = jnp.dot(values.astype(BF16), one_hot, preferred_element_type=F32)
        order[2 * n : 2 * n + 1, :] = jnp.clip(ordered[0:1].astype(jnp.int32), 0, CH - 1)
        order[2 * n + 1 : 2 * n + 2, :] = jnp.clip(ordered[1:2].astype(jnp.int32), 0, limit)
        key_s = ordered[2:3]
        before = pltpu.roll(jnp.broadcast_to(key_s, (8, SLOTS)), 1, 1)[0:1]
        same[n : n + 1, :] = jnp.where((key_s == before) & (t_lane % CH != 0), 1.0, 0.0)
        line = iota((COLS, SLOTS), 0).astype(F32)
        upto = jnp.dot(jnp.where(own <= line, 1.0, 0.0).astype(BF16), picker, preferred_element_type=F32)
        there = jnp.dot(jnp.where(own == line, 1.0, 0.0).astype(BF16), picker, preferred_element_type=F32)
        at = chunk_at * CH + upto.astype(jnp.int32) - 1
        ends[n * COLS : (n + 1) * COLS, :] = jnp.clip(jnp.where(there > 0.5, at, SLOTS), 0, SLOTS)


def tile_pass(n, c, tiles, left, order, same, run_ref):
    contract = (((1,), (1,)), ((), ())) if n == 0 else (((1,), (0,)), ((), ()))

    def step(g, run):
        for u in range(UNROLL):
            s = c * CH + g * UNROLL + u
            tile = tiles[order[2 * n, s]]
            lhs = left[order[2 * n + 1, s]]
            prod = lax.dot_general(lhs, tile, contract, preferred_element_type=F32)
            run = prod + run * same[n, s]
            run_ref[s] = run
        return run

    lax.fori_loop(0, CH // UNROLL, step, jnp.zeros((DATES, BLOCK), F32))


def gathered(n, line, run_ref, ends):
    total = run_ref[ends[n * COLS + line, 0]]
    for c in range(1, CHUNKS):
        total += run_ref[ends[n * COLS + line, c]]
    return total


def curvature_of(edges, window, base):
    e_at = iota((WIN, 2 * BLOCK), 1)
    block_at = (iota((WIN, 2 * BLOCK), 0) + base + 128 - HALO) % 128
    anchor = block_at * BLOCK + e_at // 2
    delta = edges[:, 0, :] + edges[:, 1, :] - 2 * anchor
    delta = (delta + 3 * PATCHES // 2 + PATCHES) % PATCHES - PATCHES // 2
    delta = jnp.concatenate([delta.astype(F32), jnp.zeros((16 - WIN, 2 * BLOCK), F32)], axis=0).astype(BF16)
    rows, cols = [], []
    for j in range(2):
        pick = (iota((2 * BLOCK, BLOCK), 0) == 2 * iota((2 * BLOCK, BLOCK), 1) + j).astype(F32).astype(BF16)
        pick_t = (iota((BLOCK, 2 * BLOCK), 1) == 2 * iota((BLOCK, 2 * BLOCK), 0) + j).astype(F32).astype(BF16)
        rows.append(jnp.dot(delta, pick, preferred_element_type=F32) + iota((16, BLOCK), 1).astype(F32))
        cols.append(
            lax.dot_general(pick_t, delta, (((1,), (1,)), ((), ())), preferred_element_type=F32)
            + iota((BLOCK, 16), 0).astype(F32)
        )
    q_at = iota((BLOCK, BLOCK), 1).astype(F32)
    p_at = iota((BLOCK, BLOCK), 0).astype(F32)
    smooth, middle, degree_mid = [], None, None
    for cq in range(HALO // 2, HALO // 2 + HALO + 1):
        blocks = []
        for cp in range(cq - 2, cq + 3):
            off = float((cq - cp) * BLOCK)
            adj = jnp.zeros((BLOCK, BLOCK), F32)
            for j in range(2):
                adj += jnp.where(cols[j][:, cp : cp + 1] == q_at + off, 1.0, 0.0)
                adj += jnp.where(rows[j][cq : cq + 1, :] == p_at - off, 1.0, 0.0)
            blocks.append(adj.astype(BF16))
        adj = jnp.concatenate(blocks, axis=0)
        around = jnp.dot(window[:, (cq - 2) * BLOCK : (cq + 3) * BLOCK], adj, preferred_element_type=F32)
        degree = around[DATES : DATES + 1]
        own = window[0:DATES, cq * BLOCK : (cq + 1) * BLOCK].astype(F32)
        smooth.append(degree * own - around[0:DATES])
        if cq == HALO:
            middle, degree_mid = adj, degree
    field = jnp.concatenate(smooth, axis=1)
    high = field.astype(BF16)
    low = (field - high.astype(F32)).astype(BF16)
    around = jnp.dot(high, middle, preferred_element_type=F32) + jnp.dot(low, middle, preferred_element_type=F32)
    return 0.05 * (degree_mid * smooth[HALO // 2] - around)


def kernel(
    tiles_h, row_h, col_h, count_h, slip_h, obs_h, edge_h, resid_h, grad_ref,
    tb0, tb1, tb2, tb3, row_v, col_v, count_v, slip_v, slip_blk, ext, obs_v, edges_v,
    order_v, same_v, ends_v, order, same, ends, run_ref,
    sib_send, sib_recv, chip_sum, zl_recv, resid_v, resid_blk, curve_v,
    rs_send, rs_recv, z_send, z_recv,
    tile_sem, in_sem, edge_sem, sm_sem, out_sem,
    sib_ss, sib_rs, halo_ss, halo_rs, zl_ss, zl_rs, res_ss, res_rs, rs_ss, rs_rs, z_ss, z_rs,
):
    ps, pt = lax.axis_index("ps"), lax.axis_index("patch")
    y, zh, x = ps // 16, ps // 4 % 4, ps % 4
    core = pt % 2
    par = x % 2
    tbs = (tb0, tb1, tb2, tb3)

    def at(yy, zz, xx):
        return (yy * 16 + zz * 4 + xx, pt)

    sibling = (ps, pt + 1 - 2 * core)
    across = (ps, (pt + 2) % 4)
    after = (ps, (pt + 1) % 4)
    before = (ps, (pt + 3) % 4)

    small = [
        pltpu.make_async_copy(row_h, row_v, in_sem.at[0]),
        pltpu.make_async_copy(col_h, col_v, in_sem.at[1]),
        pltpu.make_async_copy(count_h, count_v, in_sem.at[2]),
    ]
    slip_in = pltpu.make_async_copy(slip_h, slip_v, in_sem.at[3])
    for copy in small:
        copy.start()
    slip_in.start()
    tile_in = [
        pltpu.make_async_copy(tiles_h.at[pl.ds(c * CH, CH)], tbs[c], tile_sem.at[c]) for c in range(CHUNKS)
    ]
    for copy in tile_in:
        copy.start()
    obs_in = pltpu.make_async_copy(
        obs_h.at[:, pl.ds(pl.multiple_of(core * HALF, HALF), HALF)], obs_v, in_sem.at[4]
    )
    obs_in.start()
    base = pt * COLS + ps // 2
    edge_in = []
    for w in range(WIN):
        block = (base + 128 - HALO + w) % 128
        edge_in.append(
            pltpu.make_async_copy(
                edge_h.at[:, pl.ds(pl.multiple_of(block * 256, 256), 256)], edges_v.at[w], edge_sem.at[w]
            )
        )
    for copy in edge_in:
        copy.start()

    barrier = pltpu.get_barrier_semaphore()
    partners = [(ps, (pt + k) % 4) for k in (1, 2, 3)]
    partners += [at(xor(y, n), zh, xor(x, m)) for n in range(4) for m in range(4) if n or m]
    partners += [at(y, xor(zh, m), x) for m in (1, 2, 3)]
    for device in partners:
        pl.semaphore_signal(barrier, inc=1, device_id=device, device_id_type=MESH)

    for copy in small:
        copy.wait()
    sort_slots(row_v, col_v, count_v, order_v, same_v, ends_v)
    staged = [
        pltpu.make_async_copy(order_v, order, sm_sem.at[0]),
        pltpu.make_async_copy(same_v, same, sm_sem.at[1]),
        pltpu.make_async_copy(ends_v, ends, sm_sem.at[2]),
    ]
    for copy in staged:
        copy.start()
    slip_in.wait()
    for k in range(COLS):
        slip_blk[k] = slip_v[:, k * BLOCK : (k + 1) * BLOCK]
    ext[0:DATES, HALO * BLOCK : HALO * BLOCK + K_DEV] = slip_v[...]
    ext[DATES:, :] = jnp.ones((16, K_DEV + 2 * HALO * BLOCK), BF16)
    run_ref[SLOTS] = jnp.zeros((DATES, BLOCK), F32)
    for copy in staged:
        copy.wait()

    for c in range(CHUNKS):
        tile_in[c].wait()
        tile_pass(0, c, tbs[c], slip_blk, order, same, run_ref)

    pl.semaphore_wait(barrier, len(partners))

    def remote(src, dst, ss, rs, device):
        return pltpu.make_async_remote_copy(
            src_ref=src, dst_ref=dst, send_sem=ss, recv_sem=rs, device_id=device, device_id_type=MESH
        )

    sib = []
    for h in range(2):
        for k in range(4):
            sib_send[h, :, k * BLOCK : (k + 1) * BLOCK] = gathered(0, (1 - core) * 8 + h * 4 + k, run_ref, ends)
        sib.append(remote(sib_send.at[h], sib_recv.at[h], sib_ss.at[h], sib_rs.at[h], sibling))
        sib[h].start()
    halo = [
        remote(
            slip_v.at[:, pl.ds(K_DEV - HALO * BLOCK, HALO * BLOCK)],
            ext.at[pl.ds(0, DATES), pl.ds(0, HALO * BLOCK)],
            halo_ss.at[0], halo_rs.at[0], after,
        ),
        remote(
            slip_v.at[:, pl.ds(0, HALO * BLOCK)],
            ext.at[pl.ds(0, DATES), pl.ds(HALO * BLOCK + K_DEV, HALO * BLOCK)],
            halo_ss.at[1], halo_rs.at[1], before,
        ),
    ]
    zl = []
    for h in range(2):
        for k in range(4):
            chip_sum[h, :, k * BLOCK : (k + 1) * BLOCK] = gathered(0, core * 8 + h * 4 + k, run_ref, ends)
    for h in range(2):
        sib[h].wait_recv()
        chip_sum[h] = chip_sum[h] + sib_recv[h]
        zl.append(remote(chip_sum.at[h], zl_recv.at[h], zl_ss.at[h], zl_rs.at[h], across))
        zl[h].start()
    for copy in halo:
        copy.start()
    obs_in.wait()
    for copy in edge_in:
        copy.wait()

    res = []
    for h in range(2):
        zl[h].wait_recv()
        value = chip_sum[h] + zl_recv[h] - obs_v[:, h * 512 : (h + 1) * 512]
        at_h = core * 2 + h
        resid_v[at_h] = value
        res.append(remote(resid_v.at[at_h], resid_v.at[at_h], res_ss.at[h], res_rs.at[h], sibling))
        res[h].start()
        for k in range(4):
            resid_blk[at_h * 4 + k] = value[:, k * BLOCK : (k + 1) * BLOCK].astype(BF16)
    outs = []
    for h in range(2):
        res[h].wait_recv()
        at_h = (1 - core) * 2 + h
        value = resid_v[at_h]
        for k in range(4):
            resid_blk[at_h * 4 + k] = value[:, k * BLOCK : (k + 1) * BLOCK].astype(BF16)
    for q in range(4):
        outs.append(pltpu.make_async_copy(resid_v.at[q], resid_h.at[:, pl.ds(q * 512, 512)], out_sem.at[q]))
        outs[q].start()

    for c in range(CHUNKS):
        tile_pass(1, c, tbs[c], resid_blk, order, same, run_ref)

    low = iota((DATES, BLOCK), 1) < 64
    plane = {}
    for n in (2, 1, 3, 0):
        for mb in (2, 0):
            first = xor(y, n) * 8 + xor(x, mb) // 2
            for pair in range(2):
                b0 = gathered(1, first + 4 * pair, run_ref, ends)
                b1 = gathered(1, first + 4 * pair + 2, run_ref, ends)
                lanes = slice(pair * BLOCK, (pair + 1) * BLOCK)
                rs_send[n * 4 + mb + par, :, lanes] = jnp.where(low, b0, pltpu.roll(b1, 64, 1))
                rs_send[n * 4 + mb + 1 - par, :, lanes] = jnp.where(low, pltpu.roll(b0, 64, 1), b1)
            for m in (mb, mb + 1):
                if n or m:
                    i = n * 4 + m
                    plane[i] = remote(
                        rs_send.at[i], rs_recv.at[i], rs_ss.at[i], rs_rs.at[i], at(xor(y, n), zh, xor(x, m))
                    )
                    plane[i].start()

    for copy in halo:
        copy.wait_recv()
    window = ext[:, pl.ds(pl.multiple_of((ps // 2) * BLOCK, BLOCK), WIN * BLOCK)]
    curve_v[...] = curvature_of(edges_v, window, base)

    total = rs_send[0]
    for i in (1, 4, 3, 12, 5, 7, 13, 15, 2, 8, 6, 9, 14, 11, 10):
        plane[i].wait_recv()
        total = total + rs_recv[i]

    half = DATES // 2
    low_half = iota((half, BLOCK), 1) < 64

    def pack(block, odd):
        top, bottom = block[0:half], block[half:]
        if odd:
            return jnp.where(low_half, pltpu.roll(top, 64, 1), bottom)
        return jnp.where(low_half, top, pltpu.roll(bottom, 64, 1))

    for z in range(4):
        z_send[z] = pack(total[:, z // 2 * BLOCK : (z // 2 + 1) * BLOCK], z % 2)
    line = {}
    for m in (2, 1, 3):
        line[m] = remote(z_send.at[xor(zh, m)], z_recv.at[m], z_ss.at[m], z_rs.at[m], at(y, xor(zh, m), x))
        line[m].start()
    curve = curve_v[...]
    share = z_send[zh] + jnp.where(ps % 2 == 0, pack(curve, 0), pack(curve, 1))
    for m in (1, 3, 2):
        line[m].wait_recv()
        share = share + z_recv[m]
    grad_ref[0:half, :] = share[:, 0:64]
    grad_ref[half:, :] = pltpu.roll(share, 64, 1)[:, 0:64]

    for copy in outs:
        copy.wait()
    for copy in [*sib, *halo, *zl, *res, *plane.values(), *line.values()]:
        copy.wait_send()


def body(tiles, tile_row, tile_col, tile_count, slip, observations, edge_list):
    any_spec = pl.BlockSpec(memory_space=pltpu.HBM)
    vmem, dma = pltpu.VMEM, pltpu.SemaphoreType.DMA
    i32 = jnp.int32
    return pl.pallas_call(
        kernel,
        out_shape=(
            jax.ShapeDtypeStruct((DATES, ROWS * BLOCK), F32),
            jax.ShapeDtypeStruct((DATES, 64), F32),
        ),
        in_specs=[any_spec] * 7,
        out_specs=(any_spec, pl.BlockSpec(memory_space=vmem)),
        scratch_shapes=[
            *[vmem((CH, BLOCK, BLOCK), BF16) for _ in range(CHUNKS)],
            vmem((1, 1, SLOTS), i32),
            vmem((1, 1, SLOTS), i32),
            vmem((1, 1), i32),
            vmem((DATES, K_DEV), BF16),
            vmem((COLS, DATES, BLOCK), BF16),
            vmem((DATES + 16, K_DEV + 2 * HALO * BLOCK), BF16),
            vmem((DATES, HALF), F32),
            vmem((WIN, 2, 256), i32),
            vmem((8, SLOTS), i32),
            vmem((8, SLOTS), F32),
            vmem((2 * COLS, 128), i32),
            pltpu.SMEM((8, SLOTS), i32),
            pltpu.SMEM((8, SLOTS), F32),
            pltpu.SMEM((2 * COLS, 128), i32),
            vmem((SLOTS + 1, DATES, BLOCK), F32),
            vmem((2, DATES, 512), F32),
            vmem((2, DATES, 512), F32),
            vmem((2, DATES, 512), F32),
            vmem((2, DATES, 512), F32),
            vmem((4, DATES, 512), F32),
            vmem((ROWS, DATES, BLOCK), BF16),
            vmem((DATES, BLOCK), F32),
            vmem((16, DATES, 256), F32),
            vmem((16, DATES, 256), F32),
            vmem((4, DATES // 2, BLOCK), F32),
            vmem((4, DATES // 2, BLOCK), F32),
            dma((CHUNKS,)), dma((5,)), dma((WIN,)), dma((3,)), dma((4,)),
            dma((2,)), dma((2,)), dma((2,)), dma((2,)), dma((2,)), dma((2,)), dma((2,)), dma((2,)),
            dma((16,)), dma((16,)), dma((4,)), dma((4,)),
        ],
        compiler_params=pltpu.CompilerParams(
            collective_id=0, has_side_effects=True, vmem_limit_bytes=48 * 2**20
        ),
        cost_estimate=pl.CostEstimate(flops=2 * 10**9, bytes_accessed=10 * 2**20, transcendentals=0),
    )(tiles[0, 0], tile_row, tile_col, tile_count, slip, observations, edge_list)


def solution(mesh):
    in_specs = (
        P("ps", "patch", None, None, None),
        P("ps", "patch", None),
        P("ps", "patch", None),
        P("ps", "patch"),
        P(None, "patch"),
        P(None, "ps"),
        P(),
    )
    out_specs = (P(None, "ps"), P(None, ("patch", "ps")))
    return jax.shard_map(body, mesh=mesh, in_specs=in_specs, out_specs=out_specs, check_vma=False)
```

time: 583 us -> 58.1 us (0.10)
  waiting for transfers between devices: 465 us -> 0 us
  matrix products: 51.6 us -> 0 us
  Pallas kernels: 0 us -> 50.9 us
  other arithmetic: 28.3 us -> 0 us
  between operations: 15 us -> 1.3 us
  local copies, waits for them, and re-layouts: 17.9 us -> 5.65 us
    unnamed x3 -> x0, waiting for transfers between devices: 392 us -> none
    psum x1 -> x0, waiting for transfers between devices: 73.1 us -> none  [body(): predicted = lax.psum(partial_value.reshape(dates, rows_dev), 'patch')]
    dot_general x28 -> x0, matrix products: 51.6 us -> none  [the longest x1 11.7 us: body(): jnp.dot(outer_diff, outer_map, precision=HIGH, preferred_element_type=jnp...]
    pallas_call x0 -> x1, Pallas kernels: none -> 50.9 us  [body(): pl.pallas_call(kernel, out_shape=(jax.ShapeDtypeStruct((DATES, ROWS * BLO...]
    sub x4 -> x0, other arithmetic: 13.3 us -> none  [the longest x2 13.2 us: incidence(): return hits - (local_second[:, None] == columns).astype(jnp.float32)]
    and x12 -> x0, other arithmetic: 12.9 us -> none  [the longest x6 8.48 us: forward_step(): picked = jnp.take(slip_blocks, cl, axis=1)]
    gather x12 -> x0, local copies, waits for them, and re-layouts: 7.04 us -> none  [the longest x6 3.52 us: back_step(): picked = jnp.take(resid_blocks, rw, axis=1)]
  transfers between devices with their start and end apart: 4 -> 0, of which waited for: 2 -> 0; matrix products, arithmetic and copies ran while one was open for 16% -> 0% of each run, Pallas kernels for 0% -> 0%
where the time goes in v1:
time: 58.1 us; the launch traced here: 57.8 us
  Pallas kernels  50.9 us (88%)
  local copies, waits for them, and re-layouts  5.65 us (10%)
  between operations  1.3 us (2%)
    pallas_call x1, Pallas kernels, body(): pl.pallas_call(kernel, out_shape=(jax.ShapeDtypeStruct((DATES, ROWS * BLO...  50.9 us
    unnamed x12, local copies, waits for them, and re-layouts  5.65 us

profile of v1, /device:TPU:32, one launch (start us, length us, event | category | flops | bytes accessed | tf_op | source)
XLA Modules:
  0.0 57.8 jit_solution(659816936497388928)
XLA Ops:
  1.3 0.0 copy-start
  1.3 1.0 %copy-done = bf16[48,4096]{1,0:T(8,128)(2,1)S(1)} copy-done((bf16[48,4096]{1,0:T(8,128)(2,1)S(1)}, bf16[48,4096]{1,0:T(8,128)(2,1)}, u32[]{:S(2)}) %copy-start) | copy-done | bytes 393240
  2.3 0.0 copy-start.1
  2.3 1.0 %copy-done.1 = f32[48,2048]{1,0:T(8,128)S(1)} copy-done((f32[48,2048]{1,0:T(8,128)S(1)}, f32[48,2048]{1,0:T(8,128)}, u32[]{:S(2)}) %copy-start.1) | copy-done | bytes 393240
  3.3 0.0 copy-start.2
  3.3 0.9 %copy-done.2 = s32[2,32768]{1,0:T(2,128)S(1)} copy-done((s32[2,32768]{1,0:T(2,128)S(1)}, s32[2,32768]{1,0:T(2,128)}, u32[]{:S(2)}) %copy-start.2) | copy-done | bytes 262168
  4.2 0.0 copy-start.3
  4.2 0.7 %copy-done.3 = s32[1,1,256]{2,1,0:T(1,128)S(1)} copy-done((s32[1,1,256]{2,1,0:T(1,128)S(1)}, s32[1,1,256]{2,1,0:T(1,128)}, u32[]{:S(2)}) %copy-start.3) | copy-done | bytes 1048
  4.9 0.0 copy-start.4
  4.9 0.7 %copy-done.4 = s32[1,1,256]{2,1,0:T(1,128)S(1)} copy-done((s32[1,1,256]{2,1,0:T(1,128)S(1)}, s32[1,1,256]{2,1,0:T(1,128)}, u32[]{:S(2)}) %copy-start.4) | copy-done | bytes 1048
  5.6 50.9 %shard_map.86 = (f32[48,2048]{1,0:T(8,128)S(1)}, f32[48,64]{1,0:T(8,128)S(1)}) custom-call(bf16[256,128,128]{2,1,0:T(8,128)(2,1)} %bitcast.1, s32[1,1,256]{2,1,0:T(1,128)S(1)} %copy-done.3, s32[1,1,256]{2,1,0:T(1,128)S(1)} %copy-done.4, s32[1,1]{1,0:T(1,128)S(6)} %copy.11.count_h, bf16[48,4096]{1,0:T(8,128)(2,1)S(1)} %copy-done, f32[48,2048]{1,0:T(8,128)S(1)} %copy-done.1, ...), custom_call_target="tpu_custom_call" | custom-call | flops 2000000000 | bytes 10485760 | tf_op jit(solution)/shard_map/pallas_call | solution.py:348
  56.5 0.7 %copy.12 = f32[48,2048]{1,0:T(8,128)} copy(f32[48,2048]{1,0:T(8,128)S(1)} %get-tuple-element.4) | data formatting | bytes 786432
  57.2 0.6 %copy.13 = f32[48,64]{1,0:T(8,128)} copy(f32[48,64]{1,0:T(8,128)S(1)} %get-tuple-element.5) | data formatting | bytes 24576
Async XLA Ops:
  1.3 1.0 %copy-start = (bf16[48,4096]{1,0:T(8,128)(2,1)S(1)}, bf16[48,4096]{1,0:T(8,128)(2,1)}, u32[]{:S(2)}) copy-start(bf16[48,4096]{1,0:T(8,128)(2,1)} %slip_h.1) | copy-start | bytes 1179652
  2.3 1.0 %copy-start.1 = (f32[48,2048]{1,0:T(8,128)S(1)}, f32[48,2048]{1,0:T(8,128)}, u32[]{:S(2)}) copy-start(f32[48,2048]{1,0:T(8,128)} %obs_h.1) | copy-start | bytes 1179652
  3.3 0.9 %copy-start.2 = (s32[2,32768]{1,0:T(2,128)S(1)}, s32[2,32768]{1,0:T(2,128)}, u32[]{:S(2)}) copy-start(s32[2,32768]{1,0:T(2,128)} %edge_h.1) | copy-start | bytes 786436
  4.2 0.7 %copy-start.3 = (s32[1,1,256]{2,1,0:T(1,128)S(1)}, s32[1,1,256]{2,1,0:T(1,128)}, u32[]{:S(2)}) copy-start(s32[1,1,256]{2,1,0:T(1,128)} %row_h.1) | copy-start | bytes 3076
  4.9 0.7 %copy-start.4 = (s32[1,1,256]{2,1,0:T(1,128)S(1)}, s32[1,1,256]{2,1,0:T(1,128)}, u32[]{:S(2)}) copy-start(s32[1,1,256]{2,1,0:T(1,128)} %col_h.1) | copy-start | bytes 3076

commit v2 on v1

--- a/solution.py
+++ b/solution.py
@@ -1,3 +1,5 @@
+import functools
+
 import jax
 import jax.numpy as jnp
 from jax import lax
@@ -12,7 +14,7 @@
 BLOCK = 128
 DATES = 48
 SLOTS = 256
-CHUNKS = 4
+CHUNKS = 2
 CH = SLOTS // CHUNKS
 ROWS = 16
 COLS = 32
@@ -21,7 +23,7 @@
 HALO = 4
 WIN = 2 * HALO + 1
 PATCHES = 16384
-UNROLL = 8
+UNROLL = 64
 
 
 def xor(value, m):
@@ -72,16 +74,25 @@
 
 
 def tile_pass(n, c, tiles, left, order, same, run_ref):
+    zeros = jnp.zeros((DATES, BLOCK), BF16)
     contract = (((1,), (1,)), ((), ())) if n == 0 else (((1,), (0,)), ((), ()))
 
     def step(g, run):
-        for u in range(UNROLL):
+        for u in range(0, UNROLL, 2):
             s = c * CH + g * UNROLL + u
-            tile = tiles[order[2 * n, s]]
-            lhs = left[order[2 * n + 1, s]]
-            prod = lax.dot_general(lhs, tile, contract, preferred_element_type=F32)
-            run = prod + run * same[n, s]
+            pair = jnp.concatenate([tiles[order[2 * n, s]], tiles[order[2 * n, s + 1]]], axis=1 - n)
+            lhs = jnp.concatenate(
+                [
+                    jnp.concatenate([left[order[2 * n + 1, s]], zeros], axis=1),
+                    jnp.concatenate([zeros, left[order[2 * n + 1, s + 1]]], axis=1),
+                ],
+                axis=0,
+            )
+            prod = lax.dot_general(lhs, pair, contract, preferred_element_type=F32)
+            run = prod[0:DATES] + run * same[n, s]
             run_ref[s] = run
+            run = prod[DATES:] + run * same[n, s + 1]
+            run_ref[s + 1] = run
         return run
 
     lax.fori_loop(0, CH // UNROLL, step, jnp.zeros((DATES, BLOCK), F32))
@@ -138,7 +149,7 @@
 
 def kernel(
     tiles_h, row_h, col_h, count_h, slip_h, obs_h, edge_h, resid_h, grad_ref,
-    tb0, tb1, tb2, tb3, row_v, col_v, count_v, slip_v, slip_blk, ext, obs_v, edges_v,
+    tb0, tb1, row_v, col_v, count_v, slip_v, slip_blk, ext, obs_v, edges_v,
     order_v, same_v, ends_v, order, same, ends, run_ref,
     sib_send, sib_recv, chip_sum, zl_recv, resid_v, resid_blk, curve_v,
     rs_send, rs_recv, z_send, z_recv,
@@ -149,7 +160,7 @@
     y, zh, x = ps // 16, ps // 4 % 4, ps % 4
     core = pt % 2
     par = x % 2
-    tbs = (tb0, tb1, tb2, tb3)
+    tbs = (tb0, tb1)
 
     def at(yy, zz, xx):
         return (yy * 16 + zz * 4 + xx, pt)
@@ -345,6 +356,7 @@
     any_spec = pl.BlockSpec(memory_space=pltpu.HBM)
     vmem, dma = pltpu.VMEM, pltpu.SemaphoreType.DMA
     i32 = jnp.int32
+    near = functools.partial(pltpu.with_memory_space_constraint, memory_space=pltpu.HBM)
     return pl.pallas_call(
         kernel,
         out_shape=(
@@ -389,7 +401,11 @@
             collective_id=0, has_side_effects=True, vmem_limit_bytes=48 * 2**20
         ),
         cost_estimate=pl.CostEstimate(flops=2 * 10**9, bytes_accessed=10 * 2**20, transcendentals=0),
-    )(tiles[0, 0], tile_row, tile_col, tile_count, slip, observations, edge_list)
+    )(
+        *(near(a) for a in (tiles[0, 0], tile_row, tile_col)),
+        tile_count,
+        *(near(a) for a in (slip, observations, edge_list)),
+    )
 
 
 def solution(mesh):

time: 58.1 us -> 43.3 us (0.75)
  Pallas kernels: 50.9 us -> 40.6 us
  local copies, waits for them, and re-layouts: 5.65 us -> 1.36 us
    pallas_call x1, Pallas kernels: 50.9 us -> 40.6 us  [body(): pl.pallas_call(kernel, out_shape=(jax.ShapeDtypeStruct((DATES, ROWS * BLO...]
    unnamed x12 -> x2, local copies, waits for them, and re-layouts: 5.65 us -> 1.36 us
where the time goes in v2:
time: 43.3 us; the launch traced here: 43.2 us
  Pallas kernels  40.6 us (94%)
  local copies, waits for them, and re-layouts  1.36 us (3%)
  between operations  1.29 us (3%)
    pallas_call x1, Pallas kernels, body(): pl.pallas_call(kernel, out_shape=(jax.ShapeDtypeStruct((DATES, ROWS * BLO...  40.6 us
    unnamed x2, local copies, waits for them, and re-layouts  1.36 us

profile of v2, /device:TPU:32, one launch (start us, length us, event | category | flops | bytes accessed | tf_op | source)
XLA Modules:
  0.0 43.2 jit_solution(15152581106436194782)
XLA Ops:
  1.3 40.6 %shard_map.86 = (f32[48,2048]{1,0:T(8,128)S(1)}, f32[48,64]{1,0:T(8,128)S(1)}) custom-call(bf16[256,128,128]{2,1,0:T(8,128)(2,1)} %bitcast.1, s32[1,1,256]{2,1,0:T(1,128)} %row_h.1, s32[1,1,256]{2,1,0:T(1,128)} %col_h.1, s32[1,1]{1,0:T(1,128)S(6)} %copy.11.count_h, bf16[48,4096]{1,0:T(8,128)(2,1)} %slip_h.1, f32[48,2048]{1,0:T(8,128)} %obs_h.1, ...), custom_call_target="tpu_custom_call" | custom-call | flops 2000000000 | bytes 10485760 | tf_op jit(solution)/shard_map/pallas_call | solution.py:360
  41.9 0.7 %copy.12 = f32[48,2048]{1,0:T(8,128)} copy(f32[48,2048]{1,0:T(8,128)S(1)} %get-tuple-element.4) | data formatting | bytes 786432
  42.6 0.6 %copy.13 = f32[48,64]{1,0:T(8,128)} copy(f32[48,64]{1,0:T(8,128)S(1)} %get-tuple-element.5) | data formatting | bytes 24576

commit v3 on v2

--- a/solution.py
+++ b/solution.py
@@ -24,6 +24,7 @@
 WIN = 2 * HALO + 1
 PATCHES = 16384
 UNROLL = 64
+GROUPS = ((0, 16), (16, 32))
 
 
 def xor(value, m):
@@ -73,8 +74,9 @@
         ends[n * COLS : (n + 1) * COLS, :] = jnp.clip(jnp.where(there > 0.5, at, SLOTS), 0, SLOTS)
 
 
-def tile_pass(n, c, tiles, left, order, same, run_ref):
-    zeros = jnp.zeros((DATES, BLOCK), BF16)
+def tile_pass(n, c, tiles, left, order, same, run_ref, first=0, dates=DATES):
+    zeros = jnp.zeros((dates, BLOCK), BF16)
+    lines = slice(first, first + dates)
     contract = (((1,), (1,)), ((), ())) if n == 0 else (((1,), (0,)), ((), ()))
 
     def step(g, run):
@@ -89,19 +91,20 @@
                 axis=0,
             )
             prod = lax.dot_general(lhs, pair, contract, preferred_element_type=F32)
-            run = prod[0:DATES] + run * same[n, s]
-            run_ref[s] = run
-            run = prod[DATES:] + run * same[n, s + 1]
-            run_ref[s + 1] = run
+            run = prod[0:dates] + run * same[n, s]
+            run_ref[s, lines] = run
+            run = prod[dates:] + run * same[n, s + 1]
+            run_ref[s + 1, lines] = run
         return run
 
-    lax.fori_loop(0, CH // UNROLL, step, jnp.zeros((DATES, BLOCK), F32))
-
-
-def gathered(n, line, run_ref, ends):
-    total = run_ref[ends[n * COLS + line, 0]]
+    lax.fori_loop(0, CH // UNROLL, step, jnp.zeros((dates, BLOCK), F32))
+
+
+def gathered(n, line, run_ref, ends, first, dates):
+    lines = slice(first, first + dates)
+    total = run_ref[ends[n * COLS + line, 0], lines]
     for c in range(1, CHUNKS):
-        total += run_ref[ends[n * COLS + line, c]]
+        total += run_ref[ends[n * COLS + line, c], lines]
     return total
 
 
@@ -151,7 +154,7 @@
     tiles_h, row_h, col_h, count_h, slip_h, obs_h, edge_h, resid_h, grad_ref,
     tb0, tb1, row_v, col_v, count_v, slip_v, slip_blk, ext, obs_v, edges_v,
     order_v, same_v, ends_v, order, same, ends, run_ref,
-    sib_send, sib_recv, chip_sum, zl_recv, resid_v, resid_blk, curve_v,
+    sib_send, sib_recv, chip_sum, zl_recv, resid_v, resid_blk0, resid_blk1, curve_v,
     rs_send, rs_recv, z_send, z_recv,
     tile_sem, in_sem, edge_sem, sm_sem, out_sem,
     sib_ss, sib_rs, halo_ss, halo_rs, zl_ss, zl_rs, res_ss, res_rs, rs_ss, rs_rs, z_ss, z_rs,
@@ -161,6 +164,7 @@
     core = pt % 2
     par = x % 2
     tbs = (tb0, tb1)
+    resid_blks = (resid_blk0, resid_blk1)
 
     def at(yy, zz, xx):
         return (yy * 16 + zz * 4 + xx, pt)
@@ -238,11 +242,14 @@
         )
 
     sib = []
-    for h in range(2):
-        for k in range(4):
-            sib_send[h, :, k * BLOCK : (k + 1) * BLOCK] = gathered(0, (1 - core) * 8 + h * 4 + k, run_ref, ends)
-        sib.append(remote(sib_send.at[h], sib_recv.at[h], sib_ss.at[h], sib_rs.at[h], sibling))
-        sib[h].start()
+    for g, (first, dates) in enumerate(GROUPS):
+        for k in range(8):
+            sib_send[first : first + dates, k * BLOCK : (k + 1) * BLOCK] = gathered(
+                0, (1 - core) * 8 + k, run_ref, ends, first, dates
+            )
+        lines = pl.ds(first, dates)
+        sib.append(remote(sib_send.at[lines], sib_recv.at[lines], sib_ss.at[g], sib_rs.at[g], sibling))
+        sib[g].start()
     halo = [
         remote(
             slip_v.at[:, pl.ds(K_DEV - HALO * BLOCK, HALO * BLOCK)],
@@ -256,72 +263,93 @@
         ),
     ]
     zl = []
-    for h in range(2):
-        for k in range(4):
-            chip_sum[h, :, k * BLOCK : (k + 1) * BLOCK] = gathered(0, core * 8 + h * 4 + k, run_ref, ends)
-    for h in range(2):
-        sib[h].wait_recv()
-        chip_sum[h] = chip_sum[h] + sib_recv[h]
-        zl.append(remote(chip_sum.at[h], zl_recv.at[h], zl_ss.at[h], zl_rs.at[h], across))
-        zl[h].start()
+    for k in range(8):
+        chip_sum[:, k * BLOCK : (k + 1) * BLOCK] = gathered(0, core * 8 + k, run_ref, ends, 0, DATES)
+    for g, (first, dates) in enumerate(GROUPS):
+        sib[g].wait_recv()
+        lines = pl.ds(first, dates)
+        chip_sum[lines] = chip_sum[lines] + sib_recv[lines]
+        zl.append(remote(chip_sum.at[lines], zl_recv.at[lines], zl_ss.at[g], zl_rs.at[g], across))
+        zl[g].start()
     for copy in halo:
         copy.start()
     obs_in.wait()
     for copy in edge_in:
         copy.wait()
 
-    res = []
-    for h in range(2):
-        zl[h].wait_recv()
-        value = chip_sum[h] + zl_recv[h] - obs_v[:, h * 512 : (h + 1) * 512]
-        at_h = core * 2 + h
-        resid_v[at_h] = value
-        res.append(remote(resid_v.at[at_h], resid_v.at[at_h], res_ss.at[h], res_rs.at[h], sibling))
-        res[h].start()
-        for k in range(4):
-            resid_blk[at_h * 4 + k] = value[:, k * BLOCK : (k + 1) * BLOCK].astype(BF16)
-    outs = []
-    for h in range(2):
-        res[h].wait_recv()
-        at_h = (1 - core) * 2 + h
-        value = resid_v[at_h]
-        for k in range(4):
-            resid_blk[at_h * 4 + k] = value[:, k * BLOCK : (k + 1) * BLOCK].astype(BF16)
-    for q in range(4):
-        outs.append(pltpu.make_async_copy(resid_v.at[q], resid_h.at[:, pl.ds(q * 512, 512)], out_sem.at[q]))
+    res, outs, plane = [], [], {}
+
+    def own_half(g):
+        first, dates = GROUPS[g]
+        lines = pl.ds(first, dates)
+        zl[g].wait_recv()
+        value = chip_sum[lines] + zl_recv[lines] - obs_v[lines]
+        resid_v[core, lines] = value
+        res.append(
+            remote(resid_v.at[core, lines], resid_v.at[core, lines], res_ss.at[g], res_rs.at[g], sibling)
+        )
+        res[g].start()
+        for k in range(8):
+            resid_blks[g][core * 8 + k] = value[:, k * BLOCK : (k + 1) * BLOCK].astype(BF16)
+
+    def other_half(g):
+        first, dates = GROUPS[g]
+        res[g].wait_recv()
+        value = resid_v[1 - core, pl.ds(first, dates)]
+        for k in range(8):
+            resid_blks[g][(1 - core) * 8 + k] = value[:, k * BLOCK : (k + 1) * BLOCK].astype(BF16)
+
+    def to_plane(g):
+        first, dates = GROUPS[g]
+        lines = slice(first, first + dates)
+        low = iota((dates, BLOCK), 1) < 64
+        for n in (2, 1, 3, 0):
+            for mb in (2, 0):
+                line = xor(y, n) * 8 + xor(x, mb) // 2
+                for pair in range(2):
+                    b0 = gathered(1, line + 4 * pair, run_ref, ends, first, dates)
+                    b1 = gathered(1, line + 4 * pair + 2, run_ref, ends, first, dates)
+                    lanes = slice(pair * BLOCK, (pair + 1) * BLOCK)
+                    rs_send[n * 4 + mb + par, lines, lanes] = jnp.where(low, b0, pltpu.roll(b1, 64, 1))
+                    rs_send[n * 4 + mb + 1 - par, lines, lanes] = jnp.where(low, pltpu.roll(b0, 64, 1), b1)
+                for m in (mb, mb + 1):
+                    if n or m:
+                        i = n * 4 + m
+                        plane[g, i] = remote(
+                            rs_send.at[i, pl.ds(first, dates)], rs_recv.at[i, pl.ds(first, dates)],
+                            rs_ss.at[g, i], rs_rs.at[g, i], at(xor(y, n), zh, xor(x, m)),
+                        )
+                        plane[g, i].start()
+
+    def from_plane(g):
+        first, dates = GROUPS[g]
+        lines = slice(first, first + dates)
+        total = rs_send[0, lines]
+        for i in (1, 4, 3, 12, 5, 7, 13, 15, 2, 8, 6, 9, 14, 11, 10):
+            plane[g, i].wait_recv()
+            total = total + rs_recv[i, lines]
+        return total
+
+    own_half(0)
+    other_half(0)
+    tile_pass(1, 0, tbs[0], resid_blks[0], order, same, run_ref, *GROUPS[0])
+    own_half(1)
+    tile_pass(1, 1, tbs[1], resid_blks[0], order, same, run_ref, *GROUPS[0])
+    to_plane(0)
+    other_half(1)
+    for q in range(2):
+        outs.append(pltpu.make_async_copy(resid_v.at[q], resid_h.at[:, pl.ds(q * HALF, HALF)], out_sem.at[q]))
         outs[q].start()
-
     for c in range(CHUNKS):
-        tile_pass(1, c, tbs[c], resid_blk, order, same, run_ref)
-
-    low = iota((DATES, BLOCK), 1) < 64
-    plane = {}
-    for n in (2, 1, 3, 0):
-        for mb in (2, 0):
-            first = xor(y, n) * 8 + xor(x, mb) // 2
-            for pair in range(2):
-                b0 = gathered(1, first + 4 * pair, run_ref, ends)
-                b1 = gathered(1, first + 4 * pair + 2, run_ref, ends)
-                lanes = slice(pair * BLOCK, (pair + 1) * BLOCK)
-                rs_send[n * 4 + mb + par, :, lanes] = jnp.where(low, b0, pltpu.roll(b1, 64, 1))
-                rs_send[n * 4 + mb + 1 - par, :, lanes] = jnp.where(low, pltpu.roll(b0, 64, 1), b1)
-            for m in (mb, mb + 1):
-                if n or m:
-                    i = n * 4 + m
-                    plane[i] = remote(
-                        rs_send.at[i], rs_recv.at[i], rs_ss.at[i], rs_rs.at[i], at(xor(y, n), zh, xor(x, m))
-                    )
-                    plane[i].start()
+        tile_pass(1, c, tbs[c], resid_blks[1], order, same, run_ref, *GROUPS[1])
+    to_plane(1)
 
     for copy in halo:
         copy.wait_recv()
     window = ext[:, pl.ds(pl.multiple_of((ps // 2) * BLOCK, BLOCK), WIN * BLOCK)]
     curve_v[...] = curvature_of(edges_v, window, base)
 
-    total = rs_send[0]
-    for i in (1, 4, 3, 12, 5, 7, 13, 15, 2, 8, 6, 9, 14, 11, 10):
-        plane[i].wait_recv()
-        total = total + rs_recv[i]
+    total = jnp.concatenate([from_plane(0), from_plane(1)], axis=0)
 
     half = DATES // 2
     low_half = iota((half, BLOCK), 1) < 64
@@ -357,7 +385,7 @@
     vmem, dma = pltpu.VMEM, pltpu.SemaphoreType.DMA
     i32 = jnp.int32
     near = functools.partial(pltpu.with_memory_space_constraint, memory_space=pltpu.HBM)
-    return pl.pallas_call(
+    resid, grad = pl.pallas_call(
         kernel,
         out_shape=(
             jax.ShapeDtypeStruct((DATES, ROWS * BLOCK), F32),
@@ -382,12 +410,9 @@
             pltpu.SMEM((8, SLOTS), F32),
             pltpu.SMEM((2 * COLS, 128), i32),
             vmem((SLOTS + 1, DATES, BLOCK), F32),
-            vmem((2, DATES, 512), F32),
-            vmem((2, DATES, 512), F32),
-            vmem((2, DATES, 512), F32),
-            vmem((2, DATES, 512), F32),
-            vmem((4, DATES, 512), F32),
-            vmem((ROWS, DATES, BLOCK), BF16),
+            *[vmem((DATES, HALF), F32) for _ in range(4)],
+            vmem((2, DATES, HALF), F32),
+            *[vmem((ROWS, dates, BLOCK), BF16) for _, dates in GROUPS],
             vmem((DATES, BLOCK), F32),
             vmem((16, DATES, 256), F32),
             vmem((16, DATES, 256), F32),
@@ -395,7 +420,7 @@
             vmem((4, DATES // 2, BLOCK), F32),
             dma((CHUNKS,)), dma((5,)), dma((WIN,)), dma((3,)), dma((4,)),
             dma((2,)), dma((2,)), dma((2,)), dma((2,)), dma((2,)), dma((2,)), dma((2,)), dma((2,)),
-            dma((16,)), dma((16,)), dma((4,)), dma((4,)),
+            dma((2, 16)), dma((2, 16)), dma((4,)), dma((4,)),
         ],
         compiler_params=pltpu.CompilerParams(
             collective_id=0, has_side_effects=True, vmem_limit_bytes=48 * 2**20
@@ -406,6 +431,28 @@
         tile_count,
         *(near(a) for a in (slip, observations, edge_list)),
     )
+    return placed(resid, grad)
+
+
+def placed(resid, grad):
+    def copies(resid_in, grad_in, resid_out, grad_out, sem):
+        moves = [
+            pltpu.make_async_copy(resid_in, resid_out, sem.at[0]),
+            pltpu.make_async_copy(grad_in, grad_out, sem.at[1]),
+        ]
+        for move in moves:
+            move.start()
+        for move in moves:
+            move.wait()
+
+    return pl.pallas_call(
+        copies,
+        out_shape=tuple(jax.ShapeDtypeStruct(a.shape, a.dtype) for a in (resid, grad)),
+        in_specs=[pl.BlockSpec(memory_space=pl.ANY)] * 2,
+        out_specs=(pl.BlockSpec(memory_space=pl.ANY),) * 2,
+        scratch_shapes=[pltpu.SemaphoreType.DMA((2,))],
+        compiler_params=pltpu.CompilerParams(vmem_limit_bytes=2**20),
+    )(resid, grad)
 
 
 def solution(mesh):

time: 43.3 us -> 40.6 us (0.938)
  the two profiles are of different devices: /device:TPU:32 before, /device:TPU:1 now
where the time goes in v3:
time: 40.6 us; the launch traced here: 40.5 us
  Pallas kernels  39.3 us (97%)
  between operations  1.28 us (3%)
    pallas_call x1, Pallas kernels, body(): pl.pallas_call(kernel, out_shape=(jax.ShapeDtypeStruct((DATES, ROWS * BLO...  38.5 us

profile of v3, /device:TPU:1, one launch (start us, length us, event | category | flops | bytes accessed | tf_op | source)
XLA Modules:
  0.0 40.5 jit_solution(13012244047305049333)
XLA Ops:
  1.3 38.5 %shard_map.86 = (f32[48,2048]{1,0:T(8,128)S(1)}, f32[48,64]{1,0:T(8,128)S(1)}) custom-call(bf16[256,128,128]{2,1,0:T(8,128)(2,1)} %bitcast.1, s32[1,1,256]{2,1,0:T(1,128)} %row_h.1, s32[1,1,256]{2,1,0:T(1,128)} %col_h.1, s32[1,1]{1,0:T(1,128)S(6)} %copy.9.count_h, bf16[48,4096]{1,0:T(8,128)(2,1)} %slip_h.1, f32[48,2048]{1,0:T(8,128)} %obs_h.1, s32[2,32768]{1,0:T(2,128)} %edge_h.1), custom_call_target="tpu_custom_call" | custom-call | flops 2000000000 | bytes 10485760 | tf_op jit(solution)/shard_map/pallas_call | solution.py:388
  39.8 0.8 %shard_map.87 = (f32[48,2048]{1,0:T(8,128)}, f32[48,64]{1,0:T(8,128)}) custom-call(f32[48,2048]{1,0:T(8,128)S(1)} %get-tuple-element.4.resid_in, f32[48,64]{1,0:T(8,128)S(1)} %get-tuple-element.5.grad_in), custom_call_target="tpu_custom_call" | custom-call | tf_op jit(solution)/shard_map/pallas_call | solution.py:448

commit v4 on v3

--- a/solution.py
+++ b/solution.py
@@ -299,14 +299,15 @@
         for k in range(8):
             resid_blks[g][(1 - core) * 8 + k] = value[:, k * BLOCK : (k + 1) * BLOCK].astype(BF16)
 
-    def to_plane(g):
+    def to_plane(g, part, pairs):
         first, dates = GROUPS[g]
         lines = slice(first, first + dates)
         low = iota((dates, BLOCK), 1) < 64
+        lanes_sent = pl.ds(pairs[0] * BLOCK, len(pairs) * BLOCK)
         for n in (2, 1, 3, 0):
             for mb in (2, 0):
                 line = xor(y, n) * 8 + xor(x, mb) // 2
-                for pair in range(2):
+                for pair in pairs:
                     b0 = gathered(1, line + 4 * pair, run_ref, ends, first, dates)
                     b1 = gathered(1, line + 4 * pair + 2, run_ref, ends, first, dates)
                     lanes = slice(pair * BLOCK, (pair + 1) * BLOCK)
@@ -315,19 +316,21 @@
                 for m in (mb, mb + 1):
                     if n or m:
                         i = n * 4 + m
-                        plane[g, i] = remote(
-                            rs_send.at[i, pl.ds(first, dates)], rs_recv.at[i, pl.ds(first, dates)],
-                            rs_ss.at[g, i], rs_rs.at[g, i], at(xor(y, n), zh, xor(x, m)),
+                        plane[part, i] = remote(
+                            rs_send.at[i, pl.ds(first, dates), lanes_sent],
+                            rs_recv.at[i, pl.ds(first, dates), lanes_sent],
+                            rs_ss.at[part, i], rs_rs.at[part, i], at(xor(y, n), zh, xor(x, m)),
                         )
-                        plane[g, i].start()
-
-    def from_plane(g):
+                        plane[part, i].start()
+
+    def from_plane(g, part, pairs):
         first, dates = GROUPS[g]
         lines = slice(first, first + dates)
-        total = rs_send[0, lines]
+        lanes = slice(pairs[0] * BLOCK, (pairs[-1] + 1) * BLOCK)
+        total = rs_send[0, lines, lanes]
         for i in (1, 4, 3, 12, 5, 7, 13, 15, 2, 8, 6, 9, 14, 11, 10):
-            plane[g, i].wait_recv()
-            total = total + rs_recv[i, lines]
+            plane[part, i].wait_recv()
+            total = total + rs_recv[i, lines, lanes]
         return total
 
     own_half(0)
@@ -335,22 +338,22 @@
     tile_pass(1, 0, tbs[0], resid_blks[0], order, same, run_ref, *GROUPS[0])
     own_half(1)
     tile_pass(1, 1, tbs[1], resid_blks[0], order, same, run_ref, *GROUPS[0])
-    to_plane(0)
+    to_plane(0, 0, (0, 1))
     other_half(1)
     for q in range(2):
         outs.append(pltpu.make_async_copy(resid_v.at[q], resid_h.at[:, pl.ds(q * HALF, HALF)], out_sem.at[q]))
         outs[q].start()
     for c in range(CHUNKS):
         tile_pass(1, c, tbs[c], resid_blks[1], order, same, run_ref, *GROUPS[1])
-    to_plane(1)
+    to_plane(1, 1, (0,))
+    to_plane(1, 2, (1,))
 
     for copy in halo:
         copy.wait_recv()
     window = ext[:, pl.ds(pl.multiple_of((ps // 2) * BLOCK, BLOCK), WIN * BLOCK)]
     curve_v[...] = curvature_of(edges_v, window, base)
 
-    total = jnp.concatenate([from_plane(0), from_plane(1)], axis=0)
-
+    total = from_plane(0, 0, (0, 1))
     half = DATES // 2
     low_half = iota((half, BLOCK), 1) < 64
 
@@ -360,12 +363,26 @@
             return jnp.where(low_half, pltpu.roll(top, 64, 1), bottom)
         return jnp.where(low_half, top, pltpu.roll(bottom, 64, 1))
 
-    for z in range(4):
-        z_send[z] = pack(total[:, z // 2 * BLOCK : (z // 2 + 1) * BLOCK], z % 2)
     line = {}
-    for m in (2, 1, 3):
+    for m in (1, 2, 3):
         line[m] = remote(z_send.at[xor(zh, m)], z_recv.at[m], z_ss.at[m], z_rs.at[m], at(y, xor(zh, m), x))
-        line[m].start()
+
+    for pair in range(2):
+        block = jnp.concatenate(
+            [total[:, pair * BLOCK : (pair + 1) * BLOCK], from_plane(1, 1 + pair, (pair,))], axis=0
+        )
+        for odd in range(2):
+            z_send[2 * pair + odd] = pack(block, odd)
+
+        @pl.when(zh // 2 == pair)
+        def near_by():
+            line[1].start()
+
+        @pl.when(zh // 2 != pair)
+        def far():
+            line[2].start()
+            line[3].start()
+
     curve = curve_v[...]
     share = z_send[zh] + jnp.where(ps % 2 == 0, pack(curve, 0), pack(curve, 1))
     for m in (1, 3, 2):
@@ -420,7 +437,7 @@
             vmem((4, DATES // 2, BLOCK), F32),
             dma((CHUNKS,)), dma((5,)), dma((WIN,)), dma((3,)), dma((4,)),
             dma((2,)), dma((2,)), dma((2,)), dma((2,)), dma((2,)), dma((2,)), dma((2,)), dma((2,)),
-            dma((2, 16)), dma((2, 16)), dma((4,)), dma((4,)),
+            dma((3, 16)), dma((3, 16)), dma((4,)), dma((4,)),
         ],
         compiler_params=pltpu.CompilerParams(
             collective_id=0, has_side_effects=True, vmem_limit_bytes=48 * 2**20

time: 40.6 us -> 38 us (0.936)
  the two profiles are of different devices: /device:TPU:1 before, /device:TPU:32 now
where the time goes in v4:
time: 38 us; the launch traced here: 37.5 us
  Pallas kernels  36.3 us (96%)
  between operations  1.28 us (3%)
    pallas_call x1, Pallas kernels, body(): pl.pallas_call(kernel, out_shape=(jax.ShapeDtypeStruct((DATES, ROWS * BLO...  35.5 us
    pallas_call x1, Pallas kernels, placed(): pl.pallas_call(copies, out_shape=tuple((jax.ShapeDtypeStruct(a.shape, a.d...  0.77 us

profile of v4, /device:TPU:32, one launch (start us, length us, event | category | flops | bytes accessed | tf_op | source)
XLA Modules:
  0.0 37.5 jit_solution(4314111659455642008)
XLA Ops:
  1.3 35.5 %shard_map.86 = (f32[48,2048]{1,0:T(8,128)S(1)}, f32[48,64]{1,0:T(8,128)S(1)}) custom-call(bf16[256,128,128]{2,1,0:T(8,128)(2,1)} %bitcast.1, s32[1,1,256]{2,1,0:T(1,128)} %row_h.1, s32[1,1,256]{2,1,0:T(1,128)} %col_h.1, s32[1,1]{1,0:T(1,128)S(6)} %copy.9.count_h, bf16[48,4096]{1,0:T(8,128)(2,1)} %slip_h.1, f32[48,2048]{1,0:T(8,128)} %obs_h.1, s32[2,32768]{1,0:T(2,128)} %edge_h.1), custom_call_target="tpu_custom_call" | custom-call | flops 2000000000 | bytes 10485760 | tf_op jit(solution)/shard_map/pallas_call | solution.py:405
  36.8 0.8 %shard_map.87 = (f32[48,2048]{1,0:T(8,128)}, f32[48,64]{1,0:T(8,128)}) custom-call(f32[48,2048]{1,0:T(8,128)S(1)} %get-tuple-element.4.resid_in, f32[48,64]{1,0:T(8,128)S(1)} %get-tuple-element.5.grad_in), custom_call_target="tpu_custom_call" | custom-call | tf_op jit(solution)/shard_map/pallas_call | solution.py:465

commit v5 on v4

--- a/solution.py
+++ b/solution.py
@@ -41,7 +41,7 @@
     return lax.broadcasted_iota(jnp.int32, shape, dim)
 
 
-def sort_slots(row_ref, col_ref, count_ref, order, same, ends):
+def sort_slots(n, row_ref, col_ref, count_ref, order, same, ends):
     shape = (SLOTS, SLOTS)
     t_lane = iota((1, SLOTS), 1)
     live = t_lane < count_ref[...]
@@ -54,24 +54,24 @@
     which = iota((16, SLOTS), 0)
     picker = (iota((SLOTS, 128), 0) // CH == iota((SLOTS, 128), 1)).astype(BF16)
     chunk_at = iota((COLS, 128), 1)
-    for n, (mine, other, dead, limit) in enumerate(((row, col, ROWS, COLS - 1), (col, row, COLS, ROWS - 1))):
-        own = jnp.where(live, mine, dead).astype(F32)
-        key = (chunk_f * 64.0 + own) * SLOTS + t_f
-        key_col = jnp.sum(jnp.where(diagonal, key, 0.0), axis=1, keepdims=True)
-        rank = jnp.sum(jnp.where(key < key_col, 1.0, 0.0), axis=1, keepdims=True)
-        one_hot = jnp.where(rank == lane_f, 1.0, 0.0).astype(BF16)
-        values = jnp.where(which == 0, t_f - chunk_f * CH, jnp.where(which == 1, other.astype(F32), own))
-        ordered = jnp.dot(values.astype(BF16), one_hot, preferred_element_type=F32)
-        order[2 * n : 2 * n + 1, :] = jnp.clip(ordered[0:1].astype(jnp.int32), 0, CH - 1)
-        order[2 * n + 1 : 2 * n + 2, :] = jnp.clip(ordered[1:2].astype(jnp.int32), 0, limit)
-        key_s = ordered[2:3]
-        before = pltpu.roll(jnp.broadcast_to(key_s, (8, SLOTS)), 1, 1)[0:1]
-        same[n : n + 1, :] = jnp.where((key_s == before) & (t_lane % CH != 0), 1.0, 0.0)
-        line = iota((COLS, SLOTS), 0).astype(F32)
-        upto = jnp.dot(jnp.where(own <= line, 1.0, 0.0).astype(BF16), picker, preferred_element_type=F32)
-        there = jnp.dot(jnp.where(own == line, 1.0, 0.0).astype(BF16), picker, preferred_element_type=F32)
-        at = chunk_at * CH + upto.astype(jnp.int32) - 1
-        ends[n * COLS : (n + 1) * COLS, :] = jnp.clip(jnp.where(there > 0.5, at, SLOTS), 0, SLOTS)
+    mine, other, dead, limit = ((row, col, ROWS, COLS - 1), (col, row, COLS, ROWS - 1))[n]
+    own = jnp.where(live, mine, dead).astype(F32)
+    key = (chunk_f * 64.0 + own) * SLOTS + t_f
+    key_col = jnp.sum(jnp.where(diagonal, key, 0.0), axis=1, keepdims=True)
+    rank = jnp.sum(jnp.where(key < key_col, 1.0, 0.0), axis=1, keepdims=True)
+    one_hot = jnp.where(rank == lane_f, 1.0, 0.0).astype(BF16)
+    values = jnp.where(which == 0, t_f - chunk_f * CH, jnp.where(which == 1, other.astype(F32), own))
+    ordered = jnp.dot(values.astype(BF16), one_hot, preferred_element_type=F32)
+    order[0:1, :] = jnp.clip(ordered[0:1].astype(jnp.int32), 0, CH - 1)
+    order[1:2, :] = jnp.clip(ordered[1:2].astype(jnp.int32), 0, limit)
+    key_s = ordered[2:3]
+    before = pltpu.roll(jnp.broadcast_to(key_s, (8, SLOTS)), 1, 1)[0:1]
+    same[0:1, :] = jnp.where((key_s == before) & (t_lane % CH != 0), 1.0, 0.0)
+    line = iota((COLS, SLOTS), 0).astype(F32)
+    upto = jnp.dot(jnp.where(own <= line, 1.0, 0.0).astype(BF16), picker, preferred_element_type=F32)
+    there = jnp.dot(jnp.where(own == line, 1.0, 0.0).astype(BF16), picker, preferred_element_type=F32)
+    at = chunk_at * CH + upto.astype(jnp.int32) - 1
+    ends[...] = jnp.clip(jnp.where(there > 0.5, at, SLOTS), 0, SLOTS)
 
 
 def tile_pass(n, c, tiles, left, order, same, run_ref, first=0, dates=DATES):
@@ -82,29 +82,29 @@
     def step(g, run):
         for u in range(0, UNROLL, 2):
             s = c * CH + g * UNROLL + u
-            pair = jnp.concatenate([tiles[order[2 * n, s]], tiles[order[2 * n, s + 1]]], axis=1 - n)
+            pair = jnp.concatenate([tiles[order[0, s]], tiles[order[0, s + 1]]], axis=1 - n)
             lhs = jnp.concatenate(
                 [
-                    jnp.concatenate([left[order[2 * n + 1, s]], zeros], axis=1),
-                    jnp.concatenate([zeros, left[order[2 * n + 1, s + 1]]], axis=1),
+                    jnp.concatenate([left[order[1, s]], zeros], axis=1),
+                    jnp.concatenate([zeros, left[order[1, s + 1]]], axis=1),
                 ],
                 axis=0,
             )
             prod = lax.dot_general(lhs, pair, contract, preferred_element_type=F32)
-            run = prod[0:dates] + run * same[n, s]
+            run = prod[0:dates] + run * same[0, s]
             run_ref[s, lines] = run
-            run = prod[dates:] + run * same[n, s + 1]
+            run = prod[dates:] + run * same[0, s + 1]
             run_ref[s + 1, lines] = run
         return run
 
     lax.fori_loop(0, CH // UNROLL, step, jnp.zeros((dates, BLOCK), F32))
 
 
-def gathered(n, line, run_ref, ends, first, dates):
+def gathered(line, run_ref, ends, first, dates):
     lines = slice(first, first + dates)
-    total = run_ref[ends[n * COLS + line, 0], lines]
+    total = run_ref[ends[line, 0], lines]
     for c in range(1, CHUNKS):
-        total += run_ref[ends[n * COLS + line, c], lines]
+        total += run_ref[ends[line, c], lines]
     return total
 
 
@@ -153,7 +153,7 @@
 def kernel(
     tiles_h, row_h, col_h, count_h, slip_h, obs_h, edge_h, resid_h, grad_ref,
     tb0, tb1, row_v, col_v, count_v, slip_v, slip_blk, ext, obs_v, edges_v,
-    order_v, same_v, ends_v, order, same, ends, run_ref,
+    order_v0, same_v0, ends_v0, order_v1, same_v1, ends_v1, order0, same0, ends0, order1, same1, ends1, run_ref,
     sib_send, sib_recv, chip_sum, zl_recv, resid_v, resid_blk0, resid_blk1, curve_v,
     rs_send, rs_recv, z_send, z_recv,
     tile_sem, in_sem, edge_sem, sm_sem, out_sem,
@@ -164,6 +164,9 @@
     core = pt % 2
     par = x % 2
     tbs = (tb0, tb1)
+    tables_v = ((order_v0, same_v0, ends_v0), (order_v1, same_v1, ends_v1))
+    tables = ((order0, same0, ends0), (order1, same1, ends1))
+    order, same, ends = zip(*tables)
     resid_blks = (resid_blk0, resid_blk1)
 
     def at(yy, zz, xx):
@@ -213,26 +216,28 @@
 
     for copy in small:
         copy.wait()
-    sort_slots(row_v, col_v, count_v, order_v, same_v, ends_v)
-    staged = [
-        pltpu.make_async_copy(order_v, order, sm_sem.at[0]),
-        pltpu.make_async_copy(same_v, same, sm_sem.at[1]),
-        pltpu.make_async_copy(ends_v, ends, sm_sem.at[2]),
-    ]
-    for copy in staged:
-        copy.start()
+
+    def sort_by(n):
+        sort_slots(n, row_v, col_v, count_v, *tables_v[n])
+        staged = [
+            pltpu.make_async_copy(here, there, sm_sem.at[3 * n + i])
+            for i, (here, there) in enumerate(zip(tables_v[n], tables[n], strict=True))
+        ]
+        for copy in staged:
+            copy.start()
+        return staged
+
+    staged = sort_by(0)
     slip_in.wait()
     for k in range(COLS):
         slip_blk[k] = slip_v[:, k * BLOCK : (k + 1) * BLOCK]
-    ext[0:DATES, HALO * BLOCK : HALO * BLOCK + K_DEV] = slip_v[...]
-    ext[DATES:, :] = jnp.ones((16, K_DEV + 2 * HALO * BLOCK), BF16)
     run_ref[SLOTS] = jnp.zeros((DATES, BLOCK), F32)
     for copy in staged:
         copy.wait()
 
     for c in range(CHUNKS):
         tile_in[c].wait()
-        tile_pass(0, c, tbs[c], slip_blk, order, same, run_ref)
+        tile_pass(0, c, tbs[c], slip_blk, order[0], same[0], run_ref)
 
     pl.semaphore_wait(barrier, len(partners))
 
@@ -245,7 +250,7 @@
     for g, (first, dates) in enumerate(GROUPS):
         for k in range(8):
             sib_send[first : first + dates, k * BLOCK : (k + 1) * BLOCK] = gathered(
-                0, (1 - core) * 8 + k, run_ref, ends, first, dates
+                (1 - core) * 8 + k, run_ref, ends[0], first, dates
             )
         lines = pl.ds(first, dates)
         sib.append(remote(sib_send.at[lines], sib_recv.at[lines], sib_ss.at[g], sib_rs.at[g], sibling))
@@ -264,7 +269,7 @@
     ]
     zl = []
     for k in range(8):
-        chip_sum[:, k * BLOCK : (k + 1) * BLOCK] = gathered(0, core * 8 + k, run_ref, ends, 0, DATES)
+        chip_sum[:, k * BLOCK : (k + 1) * BLOCK] = gathered(core * 8 + k, run_ref, ends[0], 0, DATES)
     for g, (first, dates) in enumerate(GROUPS):
         sib[g].wait_recv()
         lines = pl.ds(first, dates)
@@ -273,8 +278,13 @@
         zl[g].start()
     for copy in halo:
         copy.start()
+    staged = sort_by(1)
+    ext[0:DATES, HALO * BLOCK : HALO * BLOCK + K_DEV] = slip_v[...]
+    ext[DATES:, :] = jnp.ones((16, K_DEV + 2 * HALO * BLOCK), BF16)
     obs_in.wait()
     for copy in edge_in:
+        copy.wait()
+    for copy in staged:
         copy.wait()
 
     res, outs, plane = [], [], {}
@@ -308,8 +318,8 @@
             for mb in (2, 0):
                 line = xor(y, n) * 8 + xor(x, mb) // 2
                 for pair in pairs:
-                    b0 = gathered(1, line + 4 * pair, run_ref, ends, first, dates)
-                    b1 = gathered(1, line + 4 * pair + 2, run_ref, ends, first, dates)
+                    b0 = gathered(line + 4 * pair, run_ref, ends[1], first, dates)
+                    b1 = gathered(line + 4 * pair + 2, run_ref, ends[1], first, dates)
                     lanes = slice(pair * BLOCK, (pair + 1) * BLOCK)
                     rs_send[n * 4 + mb + par, lines, lanes] = jnp.where(low, b0, pltpu.roll(b1, 64, 1))
                     rs_send[n * 4 + mb + 1 - par, lines, lanes] = jnp.where(low, pltpu.roll(b0, 64, 1), b1)
@@ -335,16 +345,16 @@
 
     own_half(0)
     other_half(0)
-    tile_pass(1, 0, tbs[0], resid_blks[0], order, same, run_ref, *GROUPS[0])
+    tile_pass(1, 0, tbs[0], resid_blks[0], order[1], same[1], run_ref, *GROUPS[0])
     own_half(1)
-    tile_pass(1, 1, tbs[1], resid_blks[0], order, same, run_ref, *GROUPS[0])
+    tile_pass(1, 1, tbs[1], resid_blks[0], order[1], same[1], run_ref, *GROUPS[0])
     to_plane(0, 0, (0, 1))
     other_half(1)
     for q in range(2):
         outs.append(pltpu.make_async_copy(resid_v.at[q], resid_h.at[:, pl.ds(q * HALF, HALF)], out_sem.at[q]))
         outs[q].start()
     for c in range(CHUNKS):
-        tile_pass(1, c, tbs[c], resid_blks[1], order, same, run_ref, *GROUPS[1])
+        tile_pass(1, c, tbs[c], resid_blks[1], order[1], same[1], run_ref, *GROUPS[1])
     to_plane(1, 1, (0,))
     to_plane(1, 2, (1,))
 
@@ -383,6 +393,10 @@
             line[2].start()
             line[3].start()
 
+    for copy in outs:
+        copy.wait()
+    for copy in [*sib, *halo, *zl, *res, *plane.values()]:
+        copy.wait_send()
     curve = curve_v[...]
     share = z_send[zh] + jnp.where(ps % 2 == 0, pack(curve, 0), pack(curve, 1))
     for m in (1, 3, 2):
@@ -391,9 +405,7 @@
     grad_ref[0:half, :] = share[:, 0:64]
     grad_ref[half:, :] = pltpu.roll(share, 64, 1)[:, 0:64]
 
-    for copy in outs:
-        copy.wait()
-    for copy in [*sib, *halo, *zl, *res, *plane.values(), *line.values()]:
+    for copy in line.values():
         copy.wait_send()
 
 
@@ -420,12 +432,8 @@
             vmem((DATES + 16, K_DEV + 2 * HALO * BLOCK), BF16),
             vmem((DATES, HALF), F32),
             vmem((WIN, 2, 256), i32),
-            vmem((8, SLOTS), i32),
-            vmem((8, SLOTS), F32),
-            vmem((2 * COLS, 128), i32),
-            pltpu.SMEM((8, SLOTS), i32),
-            pltpu.SMEM((8, SLOTS), F32),
-            pltpu.SMEM((2 * COLS, 128), i32),
+            *[vmem((8, SLOTS), i32), vmem((8, SLOTS), F32), vmem((COLS, 128), i32)] * 2,
+            *[pltpu.SMEM((8, SLOTS), i32), pltpu.SMEM((8, SLOTS), F32), pltpu.SMEM((COLS, 128), i32)] * 2,
             vmem((SLOTS + 1, DATES, BLOCK), F32),
             *[vmem((DATES, HALF), F32) for _ in range(4)],
             vmem((2, DATES, HALF), F32),
@@ -435,7 +443,7 @@
             vmem((16, DATES, 256), F32),
             vmem((4, DATES // 2, BLOCK), F32),
             vmem((4, DATES // 2, BLOCK), F32),
-            dma((CHUNKS,)), dma((5,)), dma((WIN,)), dma((3,)), dma((4,)),
+            dma((CHUNKS,)), dma((5,)), dma((WIN,)), dma((6,)), dma((2,)),
             dma((2,)), dma((2,)), dma((2,)), dma((2,)), dma((2,)), dma((2,)), dma((2,)), dma((2,)),
             dma((3, 16)), dma((3, 16)), dma((4,)), dma((4,)),
         ],

time: 38 us -> 37.5 us (0.987)
  no operation moved by 1% of the time
where the time goes in v5:
time: 37.5 us; the launch traced here: 37.3 us
  Pallas kernels  36 us (96%)
  between operations  1.28 us (3%)
    pallas_call x1, Pallas kernels, body(): pl.pallas_call(kernel, out_shape=(jax.ShapeDtypeStruct((DATES, ROWS * BLO...  35.2 us
    pallas_call x1, Pallas kernels, placed(): pl.pallas_call(copies, out_shape=tuple((jax.ShapeDtypeStruct(a.shape, a.d...  0.77 us

profile of v5, /device:TPU:32, one launch (start us, length us, event | category | flops | bytes accessed | tf_op | source)
XLA Modules:
  0.0 37.3 jit_solution(17011851874949256467)
XLA Ops:
  1.3 35.2 %shard_map.86 = (f32[48,2048]{1,0:T(8,128)S(1)}, f32[48,64]{1,0:T(8,128)S(1)}) custom-call(bf16[256,128,128]{2,1,0:T(8,128)(2,1)} %bitcast.1, s32[1,1,256]{2,1,0:T(1,128)} %row_h.1, s32[1,1,256]{2,1,0:T(1,128)} %col_h.1, s32[1,1]{1,0:T(1,128)S(6)} %copy.9.count_h, bf16[48,4096]{1,0:T(8,128)(2,1)} %slip_h.1, f32[48,2048]{1,0:T(8,128)} %obs_h.1, s32[2,32768]{1,0:T(2,128)} %edge_h.1), custom_call_target="tpu_custom_call" | custom-call | flops 2000000000 | bytes 10485760 | tf_op jit(solution)/shard_map/pallas_call | solution.py:417
  36.5 0.8 %shard_map.87 = (f32[48,2048]{1,0:T(8,128)}, f32[48,64]{1,0:T(8,128)}) custom-call(f32[48,2048]{1,0:T(8,128)S(1)} %get-tuple-element.4.resid_in, f32[48,64]{1,0:T(8,128)S(1)} %get-tuple-element.5.grad_in), custom_call_target="tpu_custom_call" | custom-call | tf_op jit(solution)/shard_map/pallas_call | solution.py:473

commit v6 on v5

--- a/solution.py
+++ b/solution.py
@@ -23,7 +23,7 @@
 HALO = 4
 WIN = 2 * HALO + 1
 PATCHES = 16384
-UNROLL = 64
+UNROLL = 128
 GROUPS = ((0, 16), (16, 32))
 
 

time: 37.5 us -> 37.3 us (level)
  Pallas kernels: 36 us -> 35.6 us
    pallas_call x1, Pallas kernels: 35.2 us -> 34.8 us  [body(): pl.pallas_call(kernel, out_shape=(jax.ShapeDtypeStruct((DATES, ROWS * BLO...]
where the time goes in v6:
time: 37.3 us; the launch traced here: 36.9 us
  Pallas kernels  35.6 us (95%)
  between operations  1.28 us (3%)
    pallas_call x1, Pallas kernels, body(): pl.pallas_call(kernel, out_shape=(jax.ShapeDtypeStruct((DATES, ROWS * BLO...  34.8 us
    pallas_call x1, Pallas kernels, placed(): pl.pallas_call(copies, out_shape=tuple((jax.ShapeDtypeStruct(a.shape, a.d...  0.77 us

profile of v6, /device:TPU:32, one launch (start us, length us, event | category | flops | bytes accessed | tf_op | source)
XLA Modules:
  0.0 36.9 jit_solution(11757787979426217792)
XLA Ops:
  1.3 34.8 %shard_map.86 = (f32[48,2048]{1,0:T(8,128)S(1)}, f32[48,64]{1,0:T(8,128)S(1)}) custom-call(bf16[256,128,128]{2,1,0:T(8,128)(2,1)} %bitcast.1, s32[1,1,256]{2,1,0:T(1,128)} %row_h.1, s32[1,1,256]{2,1,0:T(1,128)} %col_h.1, s32[1,1]{1,0:T(1,128)S(6)} %copy.9.count_h, bf16[48,4096]{1,0:T(8,128)(2,1)} %slip_h.1, f32[48,2048]{1,0:T(8,128)} %obs_h.1, s32[2,32768]{1,0:T(2,128)} %edge_h.1), custom_call_target="tpu_custom_call" | custom-call | flops 2000000000 | bytes 10485760 | tf_op jit(solution)/shard_map/pallas_call | solution.py:417
  36.1 0.8 %shard_map.87 = (f32[48,2048]{1,0:T(8,128)}, f32[48,64]{1,0:T(8,128)}) custom-call(f32[48,2048]{1,0:T(8,128)S(1)} %get-tuple-element.4.resid_in, f32[48,64]{1,0:T(8,128)S(1)} %get-tuple-element.5.grad_in), custom_call_target="tpu_custom_call" | custom-call | tf_op jit(solution)/shard_map/pallas_call | solution.py:473
